TPU v7x, 32 devices: a whole 2x2x4 slice. The times are simulated.
32 devices in a mesh: pole: 2 (over core), sep: 16 (over z, y, x).
Axes of the slice: x: 2, y: 2, z: 4, core: 2. Of those that a mesh axis runs over, the one named last changes fastest.
Arguments:
- diag_inverse: bfloat16 [2, 128, 2, 256, 256], P('pole', 'sep'), may hold values from -6 to 6
- coupling: bfloat16 [2, 128, 2, 256, 256], P('pole', 'sep'), may hold values from -0.25 to 0.25
- ancestor_inverse: bfloat16 [2, 16, 2, 256, 256], P('pole', 'sep'), may hold values from -6 to 6
- pole_weight: float32 [2, 2], P('pole'), may hold values from -1 to 1
- ancestor_bit: int32 [128], P('sep'), may hold values from 0 to 3
- tile_blocks: int32 [16, 6], P('sep'), may hold values from 0 to 127, as said below
- tile_count: int32 [16], P('sep'), may hold values from 1 to 6
- orbital_values: bfloat16 [16, 6, 512, 256], P('sep', None, 'pole'), may hold values from -0.375 to 0.375
Outputs:
- density_grid: float32 [16, 512], P('sep', 'pole')
Inputs may be any that keep to these rules, and one draw needn't show every extreme that they name: `tile_blocks`: entry (t, s) names a block owned by device t - 1, t or t + 1 of sep, block b being owned by device b // 8.
All inputs are finite; a program needn't handle non-finite values.
Results may differ from a plain program's by a relative error of at most 0.0035.
Values may be sent and summed in bfloat16 or wider, within the bound.
A program may use at most 64 MiB of HBM per device.

v0:
```python
import jax
import jax.numpy as jnp
from jax import lax
from jax.sharding import PartitionSpec as P

LEVELS = 4


def from_partner(x, axis, distance):
    return lax.ppermute(x, axis, [(i, i ^ 1 << distance) for i in range(lax.axis_size(axis))])


def padded(x, sides, width):
    for axis, dim in sides:
        devices, length = (lax.axis_size(axis), x.shape[dim])
        up = [(i, (i + 1) % devices) for i in range(devices - 1)]
        down = [(j, i) for i, j in up]
        last = lax.slice_in_dim(x, length - width, length, axis=dim)
        initial = lax.slice_in_dim(x, 0, width, axis=dim)
        before = lax.ppermute(last, axis, up)
        after = lax.ppermute(initial, axis, down)
        x = jnp.concatenate([before, x, after], axis=dim)
    return x


def matmul(left, right):
    return jnp.einsum("bij,bjk->bik", left, right, preferred_element_type=jnp.float32)


def matmul_t(left, right):
    return jnp.einsum("bij,bkj->bik", left, right, preferred_element_type=jnp.float32)


def shards(
    diag_inverse,
    coupling,
    ancestor_inverse,
    pole_weight,
    ancestor_bit,
    tile_blocks,
    tile_count,
    orbital_values,
):
    diag = diag_inverse[0]
    link = coupling[0]
    own_upper = ancestor_inverse[0]
    nblocks = diag.shape[0]
    chosen = jnp.zeros(diag.shape, jnp.bfloat16)
    for level in range(LEVELS):
        partner = from_partner(own_upper, "sep", level)
        chosen = jnp.where((ancestor_bit == level)[:, None, None, None], partner, chosen)
    lr, li = (link[:, 0], link[:, 1])
    gr, gi = (chosen[:, 0], chosen[:, 1])
    mr = (matmul(lr, gr) - matmul(li, gi)).astype(jnp.bfloat16)
    mi = (matmul(lr, gi) + matmul(li, gr)).astype(jnp.bfloat16)
    green_real = diag[:, 0].astype(jnp.float32) + matmul_t(mr, lr) - matmul_t(mi, li)
    green_imag = diag[:, 1].astype(jnp.float32) + matmul_t(mr, li) + matmul_t(mi, lr)
    weight = pole_weight[0]
    term = weight[0] * green_imag + weight[1] * green_real
    total = lax.psum(term, "pole").astype(jnp.bfloat16)
    near = padded(total, (("sep", 0),), nblocks)
    device = lax.axis_index("sep")
    local = tile_blocks[0] - (device - 1) * nblocks
    blocks = jnp.take(near, local, axis=0)
    values = orbital_values[0]
    inner = jnp.einsum("spw,swv->spv", values, blocks, preferred_element_type=jnp.float32)
    contribution = jnp.sum(values.astype(jnp.float32) * inner, axis=-1)
    live = (jnp.arange(values.shape[0], dtype=jnp.int32) < tile_count[0])[:, None]
    result = jnp.sum(jnp.where(live, contribution, jnp.float32(0.0)), axis=0)
    return result[None, :]


def solution(mesh):
    placed = (
        P("pole", "sep", None, None, None),
        P("pole", "sep", None, None, None),
        P("pole", "sep", None, None, None),
        P("pole", None),
        P("sep"),
        P("sep", None),
        P("sep"),
        P("sep", None, "pole", None),
    )
    return jax.shard_map(
        shards, mesh=mesh, in_specs=placed, out_specs=P("sep", "pole"), check_vma=False
    )
```

profile of v0, /device:TPU:0, one launch (start us, length us, event | category | flops | bytes accessed | tf_op | source)
XLA Modules:
  0.0 92.6 jit_solution(4846247069974182966)
XLA Ops:
  0.0 4.0 %collective-permute-start = (bf16[1,2,256,256]{3,2,1,0:T(8,128)(2,1)}, bf16[1,2,256,256]{3,2,1,0:T(8,128)(2,1)S(1)}, u32[]{:S(2)}, u32[]{:S(2)}) collective-permute-start(bf16[1,2,256,256]{3,2,1,0:T(8,128)(2,1)} %bitcast.78), channel_id=1, source_target_pairs={{0,8},{1,9},{2,10},{3,11},{4,12},{5,13},{6,14},{7,15},{8,0},{9,1},... | collective-permute-start | bytes 786440 | tf_op jit(solution)/shard_map/ppermute | solution.py:10
  4.0 1.6 %collective-permute-start.1 = (bf16[1,2,256,256]{3,2,1,0:T(8,128)(2,1)}, bf16[1,2,256,256]{3,2,1,0:T(8,128)(2,1)S(1)}, u32[]{:S(2)}, u32[]{:S(2)}) collective-permute-start(bf16[1,2,256,256]{3,2,1,0:T(8,128)(2,1)} %bitcast.79), channel_id=1, source_target_pairs={{0,4},{1,5},{2,6},{3,7},{4,0},{5,1},{6,2},{7,3},{8,12},{9,13},{10,... | collective-permute-start | bytes 786440 | tf_op jit(solution)/shard_map/ppermute | solution.py:10
  5.6 1.5 %collective-permute-start.2 = (bf16[1,2,256,256]{3,2,1,0:T(8,128)(2,1)}, bf16[1,2,256,256]{3,2,1,0:T(8,128)(2,1)S(1)}, u32[]{:S(2)}, u32[]{:S(2)}) collective-permute-start(bf16[1,2,256,256]{3,2,1,0:T(8,128)(2,1)} %bitcast.80), channel_id=1, source_target_pairs={{0,2},{1,3},{2,0},{3,1},{4,6},{5,7},{6,4},{7,5},{8,10},{9,11},{10,... | collective-permute-start | bytes 786440 | tf_op jit(solution)/shard_map/ppermute | solution.py:10
  7.1 1.5 %collective-permute-start.3 = (bf16[1,2,256,256]{3,2,1,0:T(8,128)(2,1)}, bf16[1,2,256,256]{3,2,1,0:T(8,128)(2,1)S(1)}, u32[]{:S(2)}, u32[]{:S(2)}) collective-permute-start(bf16[1,2,256,256]{3,2,1,0:T(8,128)(2,1)} %bitcast.81), channel_id=1, source_target_pairs={{0,1},{1,0},{2,3},{3,2},{4,5},{5,4},{6,7},{7,6},{8,9},{9,8},{10,11... | collective-permute-start | bytes 786440 | tf_op jit(solution)/shard_map/ppermute | solution.py:10
  8.6 1.4 %fusion.17 = (f32[1,1]{1,0:T(1,128)}, f32[1,1]{1,0:T(1,128)}) fusion(f32[1,2]{1,0:T(1,128)} %param.11), kind=kLoop, calls=%fused_computation.43 | loop fusion | bytes 16 | tf_op jit(solution)/shard_map/slice | solution.py:59
  10.0 0.0 copy-start.2
  10.0 1.9 %copy.45 = bf16[1,8,2,256,256]{4,3,1,2,0:T(8,128)(2,1)S(1)} copy(bf16[1,8,2,256,256]{4,3,2,1,0:T(8,128)(2,1)} %param.9) | data formatting | bytes 4194304 | tf_op args[1]
  11.9 0.3 copy-done.2
  12.2 0.0 copy-start.5
  12.2 1.5 %copy.46 = bf16[1,8,2,256,256]{4,3,1,2,0:T(8,128)(2,1)} copy(bf16[1,8,2,256,256]{4,3,2,1,0:T(8,128)(2,1)S(1)} %copy-done.2) | data formatting | bytes 4194304 | tf_op args[0]
  13.7 0.0 copy-done.5
  13.7 2.5 %collective-permute-done = bf16[1,2,256,256]{3,2,1,0:T(8,128)(2,1)S(1)} collective-permute-done((bf16[1,2,256,256]{3,2,1,0:T(8,128)(2,1)}, bf16[1,2,256,256]{3,2,1,0:T(8,128)(2,1)S(1)}, u32[]{:S(2)}, u32[]{:S(2)}) %collective-permute-start) | collective-permute-done | bytes 262176 | tf_op jit(solution)/shard_map/ppermute | solution.py:10
  16.3 0.1 copy.24
  16.4 0.0 collective-permute-done.1
  16.5 0.1 copy.25
  16.6 0.0 collective-permute-done.2
  16.6 0.1 copy.26
  16.8 0.0 collective-permute-done.3
  16.8 0.1 copy.27
  16.9 0.6 select_select_fusion
  17.5 0.5 fusion.7
  18.0 0.5 fusion.6
  18.5 0.5 subtract_convert_fusion
  19.0 0.5 fusion.13
  19.5 0.5 fusion.11
  20.0 0.5 add_convert_fusion
  20.5 0.0 copy-start
  20.5 0.5 fusion.12
  21.0 1.1 %copy-done = bf16[1,8,2,256,256]{4,3,1,2,0:T(8,128)(2,1)S(1)} copy-done((bf16[1,8,2,256,256]{4,3,1,2,0:T(8,128)(2,1)S(1)}, bf16[1,8,2,256,256]{4,3,1,2,0:T(8,128)(2,1)}, u32[]{:S(2)}) %copy-start) | copy-done | bytes 2097176
  22.1 3.5 %fusion.2 = f32[8,256,256]{2,1,0:T(8,128)} fusion(f32[8,256,256]{2,1,0:T(8,128)S(1)} %fusion.11, f32[8,256,256]{2,1,0:T(8,128)S(1)} %fusion.12, f32[8,256,256]{2,1,0:T(8,128)S(1)} %fusion.13, bf16[8,256,256]{2,1,0:T(8,128)(2,1)S(1)} %add_convert_fusion, bf16[8,2,256,256]{3,2,0,1:T(8,128)(2,1)S(1)} %bitcast.73, f32[]{:T(128)} %bitcast.16, f32[]{:T(128)} %bitcast.3, ...), kind=kOutput, calls=%fused_computation.5 | convolution fusion | flops 273154048 | bytes 12582920 | tf_op jit(solution)/shard_map/bij,bkj->bik/dot_general | solution.py:31
  25.6 0.0 copy-start.4
  25.6 0.0 copy-start.6
  25.6 9.7 %all-reduce.1 = bf16[8,256,256]{2,1,0:T(8,128)(2,1)S(1)} all-reduce(f32[8,256,256]{2,1,0:T(8,128)} %fusion.2), channel_id=1, replica_groups=mesh['pole'=2,'sep'=16] {'pole'}, use_global_device_ids=true, to_apply=%region_0.1 | all-reduce | flops 524288 | bytes 3145728 | tf_op jit(solution)/shard_map/psum | solution.py:60
  35.4 0.0 copy-start.1
  35.4 3.5 %collective-permute-start.4 = (bf16[8,256,256]{2,1,0:T(8,128)(2,1)S(1)}, bf16[8,256,256]{2,1,0:T(8,128)(2,1)S(1)}, u32[]{:S(2)}, u32[]{:S(2)}) collective-permute-start(bf16[8,256,256]{2,1,0:T(8,128)(2,1)S(1)} %all-reduce.1), channel_id=1, source_target_pairs={{0,1},{1,2},{2,3},{3,4},{4,5},{5,6},{6,7},{7,8},{8,9},{9,10},{10,1... | collective-permute-start | bytes 3145736 | tf_op jit(solution)/shard_map/ppermute | solution.py:20
  38.9 1.3 %collective-permute-start.5 = (bf16[8,256,256]{2,1,0:T(8,128)(2,1)S(1)}, bf16[8,256,256]{2,1,0:T(8,128)(2,1)}, u32[]{:S(2)}, u32[]{:S(2)}) collective-permute-start(bf16[8,256,256]{2,1,0:T(8,128)(2,1)S(1)} %all-reduce.1), channel_id=1, source_target_pairs={{1,0},{2,1},{3,2},{4,3},{5,4},{6,5},{7,6},{8,7},{9,8},{10,9},{11,1... | collective-permute-start | bytes 3145736 | tf_op jit(solution)/shard_map/ppermute | solution.py:21
  40.2 0.0 copy-done.4
  40.2 1.2 %copy.22 = bf16[1,6,256,256]{2,3,1,0:T(8,128)(2,1)} copy(bf16[1,6,256,256]{3,2,1,0:T(8,128)(2,1)S(1)} %copy-done.4) | data formatting | bytes 1572864 | tf_op args[7]
  42.0 0.0 copy-done.6
  42.1 42.1 %collective-permute-done.4 = bf16[8,256,256]{2,1,0:T(8,128)(2,1)S(1)} collective-permute-done((bf16[8,256,256]{2,1,0:T(8,128)(2,1)S(1)}, bf16[8,256,256]{2,1,0:T(8,128)(2,1)S(1)}, u32[]{:S(2)}, u32[]{:S(2)}) %collective-permute-start.4) | collective-permute-done | bytes 1048608 | tf_op jit(solution)/shard_map/ppermute | solution.py:20
  84.2 0.0 copy-done.1
  84.2 0.0 copy-start.3
  84.2 1.0 %copy-done.3 = bf16[8,256,256]{2,1,0:T(8,128)(2,1)} copy-done((bf16[8,256,256]{2,1,0:T(8,128)(2,1)}, bf16[8,256,256]{2,1,0:T(8,128)(2,1)S(1)}, u32[]{:S(2)}) %copy-start.3) | copy-done | bytes 1048600
  85.2 1.0 %collective-permute-done.5 = bf16[8,256,256]{2,1,0:T(8,128)(2,1)} collective-permute-done((bf16[8,256,256]{2,1,0:T(8,128)(2,1)S(1)}, bf16[8,256,256]{2,1,0:T(8,128)(2,1)}, u32[]{:S(2)}, u32[]{:S(2)}) %collective-permute-start.5) | collective-permute-done | bytes 1048608 | tf_op jit(solution)/shard_map/ppermute | solution.py:21
  86.3 2.0 %pad_maximum_fusion = bf16[24,256,256]{2,1,0:T(8,128)(2,1)S(1)} fusion(bf16[8,256,256]{2,1,0:T(8,128)(2,1)} %collective-permute-done.5, bf16[8,256,256]{2,1,0:T(8,128)(2,1)} %copy-done.1, bf16[8,256,256]{2,1,0:T(8,128)(2,1)} %copy-done.3), kind=kLoop, calls=%fused_computation.1 | loop fusion | flops 3145728 | bytes 6291456 | tf_op jit(solution)/shard_map/concatenate | solution.py:22
  88.3 1.5 %gather_fusion = bf16[6,256,256]{2,1,0:T(8,128)(2,1)} fusion(bf16[24,256,256]{2,1,0:T(8,128)(2,1)S(1)} %pad_maximum_fusion, s32[1024]{0:T(1024)S(1)} %pad_clamp_fusion), kind=kCustom, calls=%fused_computation | custom fusion | bytes 1572888 | tf_op jit(solution)/shard_map/jit(_take)/gather | solution.py:64
  89.8 2.1 %fusion.5 = f32[6,256]{1,0:T(8,128)S(1)} fusion(bf16[1,6,256,256]{3,2,1,0:T(8,128)(2,1)} %param.15, bf16[1,6,256,256]{2,3,1,0:T(8,128)(2,1)} %copy.22, bf16[6,256,256]{2,1,0:T(8,128)(2,1)} %gather_fusion, pred[6]{0:T(512)(128)(4,1)S(1)} %compare_and_fusion), kind=kOutput, calls=%fused_computation.15 | convolution fusion | flops 202897920 | bytes 2365446 | tf_op jit(solution)/shard_map/spw,swv->spv/dot_general | solution.py:66
  92.0 0.6 select_reduce_fusion
  (5 shorter events, 0.0 us)
Async XLA Ops:
  0.0 16.3 %collective-permute-start = (bf16[1,2,256,256]{3,2,1,0:T(8,128)(2,1)}, bf16[1,2,256,256]{3,2,1,0:T(8,128)(2,1)S(1)}, u32[]{:S(2)}, u32[]{:S(2)}) collective-permute-start(bf16[1,2,256,256]{3,2,1,0:T(8,128)(2,1)} %bitcast.78), channel_id=1, source_target_pairs={{0,8},{1,9},{2,10},{3,11},{4,12},{5,13},{6,14},{7,15},{8,0},{9,1},... | collective-permute-start | bytes 786440 | tf_op jit(solution)/shard_map/ppermute | solution.py:10
  4.0 12.4 %collective-permute-start.1 = (bf16[1,2,256,256]{3,2,1,0:T(8,128)(2,1)}, bf16[1,2,256,256]{3,2,1,0:T(8,128)(2,1)S(1)}, u32[]{:S(2)}, u32[]{:S(2)}) collective-permute-start(bf16[1,2,256,256]{3,2,1,0:T(8,128)(2,1)} %bitcast.79), channel_id=1, source_target_pairs={{0,4},{1,5},{2,6},{3,7},{4,0},{5,1},{6,2},{7,3},{8,12},{9,13},{10,... | collective-permute-start | bytes 786440 | tf_op jit(solution)/shard_map/ppermute | solution.py:10
  5.6 11.0 %collective-permute-start.2 = (bf16[1,2,256,256]{3,2,1,0:T(8,128)(2,1)}, bf16[1,2,256,256]{3,2,1,0:T(8,128)(2,1)S(1)}, u32[]{:S(2)}, u32[]{:S(2)}) collective-permute-start(bf16[1,2,256,256]{3,2,1,0:T(8,128)(2,1)} %bitcast.80), channel_id=1, source_target_pairs={{0,2},{1,3},{2,0},{3,1},{4,6},{5,7},{6,4},{7,5},{8,10},{9,11},{10,... | collective-permute-start | bytes 786440 | tf_op jit(solution)/shard_map/ppermute | solution.py:10
  7.1 9.6 %collective-permute-start.3 = (bf16[1,2,256,256]{3,2,1,0:T(8,128)(2,1)}, bf16[1,2,256,256]{3,2,1,0:T(8,128)(2,1)S(1)}, u32[]{:S(2)}, u32[]{:S(2)}) collective-permute-start(bf16[1,2,256,256]{3,2,1,0:T(8,128)(2,1)} %bitcast.81), channel_id=1, source_target_pairs={{0,1},{1,0},{2,3},{3,2},{4,5},{5,4},{6,7},{7,6},{8,9},{9,8},{10,11... | collective-permute-start | bytes 786440 | tf_op jit(solution)/shard_map/ppermute | solution.py:10
  10.0 2.2 %copy-start.2 = (bf16[1,8,2,256,256]{4,3,2,1,0:T(8,128)(2,1)S(1)}, bf16[1,8,2,256,256]{4,3,2,1,0:T(8,128)(2,1)}, u32[]{:S(2)}) copy-start(bf16[1,8,2,256,256]{4,3,2,1,0:T(8,128)(2,1)} %param.8) | copy-start | bytes 6291460
  12.2 1.5 %copy-start.5 = (s32[8]{0:T(128)S(1)}, s32[8]{0:T(128)}, u32[]{:S(2)}) copy-start(s32[8]{0:T(128)} %param.12) | copy-start | bytes 100
  20.5 1.6 %copy-start = (bf16[1,8,2,256,256]{4,3,1,2,0:T(8,128)(2,1)S(1)}, bf16[1,8,2,256,256]{4,3,1,2,0:T(8,128)(2,1)}, u32[]{:S(2)}) copy-start(bf16[1,8,2,256,256]{4,3,1,2,0:T(8,128)(2,1)} %copy.46) | copy-start | bytes 6291460
  25.6 14.6 %copy-start.4 = (bf16[1,6,256,256]{3,2,1,0:T(8,128)(2,1)S(1)}, bf16[1,6,256,256]{3,2,1,0:T(8,128)(2,1)}, u32[]{:S(2)}) copy-start(bf16[1,6,256,256]{3,2,1,0:T(8,128)(2,1)} %param.15) | copy-start | bytes 2359300
  25.6 16.4 %copy-start.6 = (s32[1,6]{1,0:T(1,128)S(1)}, s32[1,6]{1,0:T(1,128)}, u32[]{:S(2)}) copy-start(s32[1,6]{1,0:T(1,128)} %param.13) | copy-start | bytes 76
  35.4 48.9 %copy-start.1 = (bf16[8,256,256]{2,1,0:T(8,128)(2,1)}, bf16[8,256,256]{2,1,0:T(8,128)(2,1)S(1)}, u32[]{:S(2)}) copy-start(bf16[8,256,256]{2,1,0:T(8,128)(2,1)S(1)} %all-reduce.1) | copy-start | bytes 3145732
  35.4 48.9 %collective-permute-start.4 = (bf16[8,256,256]{2,1,0:T(8,128)(2,1)S(1)}, bf16[8,256,256]{2,1,0:T(8,128)(2,1)S(1)}, u32[]{:S(2)}, u32[]{:S(2)}) collective-permute-start(bf16[8,256,256]{2,1,0:T(8,128)(2,1)S(1)} %all-reduce.1), channel_id=1, source_target_pairs={{0,1},{1,2},{2,3},{3,4},{4,5},{5,6},{6,7},{7,8},{8,9},{9,10},{10,1... | collective-permute-start | bytes 3145736 | tf_op jit(solution)/shard_map/ppermute | solution.py:20
  38.9 47.4 %collective-permute-start.5 = (bf16[8,256,256]{2,1,0:T(8,128)(2,1)S(1)}, bf16[8,256,256]{2,1,0:T(8,128)(2,1)}, u32[]{:S(2)}, u32[]{:S(2)}) collective-permute-start(bf16[8,256,256]{2,1,0:T(8,128)(2,1)S(1)} %all-reduce.1), channel_id=1, source_target_pairs={{1,0},{2,1},{3,2},{4,3},{5,4},{6,5},{7,6},{8,7},{9,8},{10,9},{11,1... | collective-permute-start | bytes 3145736 | tf_op jit(solution)/shard_map/ppermute | solution.py:21
  84.2 1.0 %copy-start.3 = (bf16[8,256,256]{2,1,0:T(8,128)(2,1)}, bf16[8,256,256]{2,1,0:T(8,128)(2,1)S(1)}, u32[]{:S(2)}) copy-start(bf16[8,256,256]{2,1,0:T(8,128)(2,1)S(1)} %collective-permute-done.4) | copy-start | bytes 3145732
where the time goes:
time: 92.9 us; the launch traced here: 92.6 us
  waiting for transfers between devices  45.8 us (49%)
  starting transfers between devices  13.5 us (15%)
  local copies, waits for them, and re-layouts  10.4 us (11%)
  blocking collectives  9.71 us (10%)
  matrix products  9.08 us (10%)
  other arithmetic  3.33 us (4%)
    ppermute x1, waiting for transfers between devices, padded(): before = lax.ppermute(last, axis, up)  42.1 us
    psum x1, blocking collectives, shards(): total = lax.psum(term, 'pole').astype(jnp.bfloat16)  9.71 us
    ppermute x4, starting transfers between devices, from_partner(): lax.ppermute(x, axis, [(i, i ^ 1 << distance) for i in range(lax.axis_siz...  8.62 us
    unnamed x17, local copies, waits for them, and re-layouts  6.97 us
    dot_general x4, matrix products, matmul_t(): jnp.einsum('bij,bkj->bik', left, right, preferred_element_type=jnp.float32)  5.04 us
    ppermute x1, starting transfers between devices, padded(): before = lax.ppermute(last, axis, up)  3.54 us
    ppermute x4, waiting for transfers between devices, from_partner(): lax.ppermute(x, axis, [(i, i ^ 1 << distance) for i in range(lax.axis_siz...  2.6 us
    dot_general x1, matrix products, shards(): jnp.einsum('spw,swv->spv', values, blocks, preferred_element_type=jnp.flo...  2.12 us
  transfers between devices with their start and end apart: 6, of which 3 were waited for; matrix products, arithmetic and copies ran while one was open for 7% of the time, Pallas kernels for 0%

commit v1 on v0

v1 whole, which is shorter than its diff:
```python
import functools

import jax
import jax.numpy as jnp
from jax import lax
from jax.experimental import pallas as pl
from jax.experimental.pallas import tpu as pltpu
from jax.sharding import PartitionSpec as P

LEVELS = 4
CHUNKS = 2
MESH = pl.DeviceIdType.MESH
F32 = jnp.float32
BF16 = jnp.bfloat16


def nt_dot(left, right):
    return lax.dot_general(left, right, (((1,), (1,)), ((), ())), preferred_element_type=F32)


def kernel(
    n_pole,
    n_sep,
    weight_ref,
    bit_ref,
    blocks_ref,
    count_ref,
    diag_hbm,
    link_hbm,
    upper_hbm,
    values_hbm,
    out_ref,
    diag,
    link,
    upper,
    values,
    packed,
    arrived,
    full,
    body,
    body_diag,
    part_send,
    part_recv,
    part_diag,
    mine,
    own,
    near,
    near_diag,
    chosen,
    list_send,
    list_recv,
    list_smem,
    local_sem,
    list_sem,
    upper_send_sem,
    upper_recv_sem,
    part_send_sem,
    part_recv_sem,
    pdiag_send_sem,
    pdiag_recv_sem,
    own_send_sem,
    own_recv_sem,
    halo_send_sem,
    halo_recv_sem,
    hdiag_send_sem,
    hdiag_recv_sem,
    fwd_send_sem,
    fwd_recv_sem,
    list_send_sem,
    list_recv_sem,
):
    pole = lax.axis_index("pole")
    me = lax.axis_index("sep")
    nblocks = link.shape[0]
    slots = values.shape[0]
    half = packed.shape[1]
    rows = mine.shape[1]
    per_chunk = nblocks // CHUNKS
    peers = range(1, n_pole)

    def peer(k):
        return lax.rem(pole + k, n_pole)

    def piece(q):
        return pl.ds(pl.multiple_of(q * rows, rows), rows)

    def partner(level):
        step = 2**level
        return me + step * (1 - 2 * lax.rem(me // step, 2))

    sides = ((0, me > 0, me - 1), (1, me < n_sep - 1, me + 1))

    def remote(src, dst, send, recv, where):
        return pltpu.make_async_remote_copy(
            src_ref=src, dst_ref=dst, send_sem=send, recv_sem=recv, device_id=where, device_id_type=MESH
        )

    loads = [
        pltpu.make_async_copy(src, dst, local_sem.at[i])
        for i, (src, dst) in enumerate(
            (
                (upper_hbm.at[0, 0], upper),
                (diag_hbm.at[0], diag),
                (link_hbm.at[0], link),
                (values_hbm.at[0], values),
            )
        )
    ]
    for load in loads:
        load.start()

    barrier = pltpu.get_barrier_semaphore()
    for k in peers:
        pl.semaphore_signal(barrier, inc=1, device_id={"pole": peer(k)}, device_id_type=MESH)
    for level in range(LEVELS):
        pl.semaphore_signal(barrier, inc=1, device_id={"sep": partner(level)}, device_id_type=MESH)
    for _, there, neighbour in sides:

        @pl.when(there)
        def _():
            pl.semaphore_signal(barrier, inc=1, device_id={"sep": neighbour}, device_id_type=MESH)

    row = lax.broadcasted_iota(jnp.int32, (half, half), 0)
    col = lax.broadcasted_iota(jnp.int32, (half, half), 1)
    above, below, on = row < col, row > col, row == col

    def diagonal(x):
        return jnp.sum(jnp.where(on, x, 0.0), axis=0, keepdims=True)

    wr, wi = weight_ref[0, 0], weight_ref[0, 1]

    lane = lax.broadcasted_iota(jnp.int32, list_send.shape, 1)
    listed = jnp.zeros(list_send.shape, jnp.int32)
    for s in range(slots):
        listed = jnp.where(lane == s, blocks_ref[0, s], listed)
    list_send[...] = listed

    loads[0].wait()
    doubled = []
    for part in range(2):
        g00 = upper[part, :half, :half].astype(F32)
        g01 = upper[part, :half, half:].astype(F32)
        g10 = upper[part, half:, :half].astype(F32)
        g11 = upper[part, half:, half:].astype(F32)
        doubled.append((g00 + g00.T, g01 + g10.T, g11 + g11.T))
    weighted = (
        [wr * a - wi * b for a, b in zip(*doubled)],
        [wr * b + wi * a for a, b in zip(*doubled)],
    )
    ends = []
    for part in range(2):
        s00, s01, s11 = weighted[part]
        packed[2 * part] = s01.astype(BF16)
        packed[2 * part + 1] = jnp.where(below, s11, s00).astype(BF16)
        ends.append(diagonal(s11))
    packed[4] = jnp.where(row == 0, ends[0], jnp.where(row == 1, ends[1], 0.0)).astype(BF16)

    pl.semaphore_wait(
        barrier, n_pole - 1 + LEVELS + (me > 0).astype(jnp.int32) + (me < n_sep - 1).astype(jnp.int32)
    )

    def upper_copies(level):
        where = {"sep": partner(level)}
        return (
            remote(
                packed.at[pl.ds(0, 4)],
                arrived.at[level, pl.ds(0, 4)],
                upper_send_sem.at[level, 0],
                upper_recv_sem.at[level, 0],
                where,
            ),
            remote(
                packed.at[4, pl.ds(0, 16)],
                arrived.at[level, 4, pl.ds(0, 16)],
                upper_send_sem.at[level, 1],
                upper_recv_sem.at[level, 1],
                where,
            ),
        )

    for level in reversed(range(LEVELS)):
        for copy in upper_copies(level):
            copy.start()

    def list_copy(d, neighbour, slot):
        return remote(
            list_send, list_recv.at[slot], list_send_sem.at[d], list_recv_sem.at[slot], {"sep": neighbour}
        )

    for d, there, neighbour in sides:

        @pl.when(there)
        def _():
            list_copy(d, neighbour, 1 - d).start()

    loads[1].wait()

    def fold(b, carry):
        def term(rows_at, cols_at):
            real = diag[b, 0, rows_at, cols_at].astype(F32)
            imag = diag[b, 1, rows_at, cols_at].astype(F32)
            return wr * imag + wi * real

        low, high = pl.ds(0, half), pl.ds(half, half)
        t00, t01, t10, t11 = term(low, low), term(low, high), term(high, low), term(high, high)
        body[b, :half, :] = t01 + t10.T
        body[b, half:, :] = jnp.where(above, t00 + t00.T, jnp.where(below, t11 + t11.T, t00))
        body_diag[pl.ds(b, 1), :] = diagonal(t11)
        return carry

    lax.fori_loop(0, nblocks, fold, 0)
    loads[2].wait()

    for d, there, neighbour in sides:

        @pl.when(there)
        def _():
            list_copy(d, neighbour, d).wait_recv()
            fetch = pltpu.make_async_copy(list_recv.at[d], list_smem.at[d], list_sem.at[d])
            fetch.start()
            fetch.wait()

    for level in range(LEVELS):
        for copy in upper_copies(level):
            copy.wait_recv()
        ends = arrived[level, 4, :16, :].astype(F32)
        symmetric = []
        for part in range(2):
            u01 = arrived[level, 2 * part]
            both = arrived[level, 2 * part + 1].astype(F32)
            turned = both.T
            g00 = jnp.where(below, turned, both)
            g11 = jnp.where(below, both, jnp.where(above, turned, ends[part : part + 1, :]))
            u10 = u01.astype(F32).T.astype(BF16)
            symmetric.append(((g00.astype(BF16), u01), (u10, g11.astype(BF16))))
        for i in range(2):
            for j in range(2):
                real, imag = symmetric[0][i][j], symmetric[1][i][j]
                r, c = i * half, j * half
                full[level, r : r + half, c : c + half] = real
                full[level, r : r + half, 2 * half + c : 3 * half + c] = imag
                full[level, 2 * half + r : 3 * half + r, c : c + half] = -imag
                full[level, 2 * half + r : 3 * half + r, 2 * half + c : 3 * half + c] = real

    def density(b, carry):
        real, imag = link[b, 0], link[b, 1]
        middle = jnp.dot(
            jnp.concatenate([real, imag], axis=1), full[bit_ref[b]], preferred_element_type=F32
        ).astype(BF16)
        crossed = jnp.concatenate([imag, real], axis=1)
        top = nt_dot(middle[:half], crossed)
        low = nt_dot(middle[half:], crossed[half:])
        corner = top[:, :half]
        body[b, :half, :] += top[:, half:]
        body[b, half:, :] += jnp.where(above, corner, jnp.where(below, low, 0.5 * corner))
        body_diag[pl.ds(b, 1), :] += 0.5 * diagonal(low)
        return carry

    def part_copy(chunk, k):
        at = pl.ds(chunk * per_chunk, per_chunk)
        return remote(
            part_send.at[k, at],
            part_recv.at[k, at],
            part_send_sem.at[chunk, k],
            part_recv_sem.at[chunk, k],
            {"pole": peer(k)},
        )

    def pdiag_copy(k):
        return remote(
            body_diag, part_diag.at[k], pdiag_send_sem.at[k], pdiag_recv_sem.at[k], {"pole": peer(k)}
        )

    for chunk in range(CHUNKS):
        lax.fori_loop(chunk * per_chunk, (chunk + 1) * per_chunk, density, 0)
        for k in peers:
            at = pl.ds(chunk * per_chunk, per_chunk)
            part_send[k, at] = body[at, piece(peer(k)), :]
            part_copy(chunk, k).start()
    for k in peers:
        pdiag_copy(k).start()

    for chunk in range(CHUNKS):
        at = pl.ds(chunk * per_chunk, per_chunk)
        total = body[at, piece(pole), :]
        for k in peers:
            part_copy(chunk, k).wait_recv()
            total = total + part_recv[k, at]
        mine[at] = total.astype(BF16)

    def halo_copy(d, neighbour, slot, s):
        return remote(
            chosen.at[d, s],
            near.at[slot, s, piece(pole)],
            halo_send_sem.at[d, s],
            halo_recv_sem.at[slot, s],
            {"sep": neighbour},
        )

    for s in range(slots):
        for d, there, neighbour in sides:

            @pl.when(there)
            def _():
                local = jnp.clip(list_smem[d, 0, s] - me * nblocks, 0, nblocks - 1)
                chosen[d, s] = mine[local]
                halo_copy(d, neighbour, 1 - d, s).start()

    def own_copy(k, q):
        return remote(
            mine, own.at[:, piece(q)], own_send_sem.at[k], own_recv_sem.at[k], {"pole": peer(k)}
        )

    for k in peers:
        own_copy(k, pole).start()
    own[:, piece(pole), :] = mine[...]

    ends = body_diag[...]
    for k in peers:
        pdiag_copy(k).wait_recv()
        ends = ends + part_diag[k]
    near_diag[1] = ends

    def hdiag_copy(d, neighbour, slot):
        return remote(
            near_diag.at[1],
            near_diag.at[2 * slot],
            hdiag_send_sem.at[d],
            hdiag_recv_sem.at[slot],
            {"sep": neighbour},
        )

    for d, there, neighbour in sides:

        @pl.when(there)
        def _():
            hdiag_copy(d, neighbour, 1 - d).start()

    loads[3].wait()
    for k in peers:
        own_copy(k, peer(n_pole - k)).wait_recv()
    for d, there, neighbour in sides:

        @pl.when(there)
        def _():
            hdiag_copy(d, neighbour, d).wait_recv()

    def fwd_copy(d, s, k, q):
        return remote(
            near.at[d, s, piece(pole)],
            near.at[d, s, piece(q)],
            fwd_send_sem.at[d, s, k],
            fwd_recv_sem.at[d, s, k],
            {"pole": peer(k)},
        )

    def forward(s):
        for d, there, neighbour in sides:

            @pl.when(there)
            def _():
                halo_copy(d, neighbour, d, s).wait_recv()
                for k in peers:
                    fwd_copy(d, s, k, pole).start()

    def contribution(s):
        for d, there, _ in sides:

            @pl.when(there)
            def _():
                for k in peers:
                    fwd_copy(d, s, k, peer(n_pole - k)).wait_recv()

        local = blocks_ref[0, s] - me * nblocks
        inside = jnp.clip(local, 0, nblocks - 1)
        block = jnp.where(local < 0, near[0, s], jnp.where(local < nblocks, own[inside], near[1, s]))
        before, here, after = (near_diag[i, pl.ds(j, 1), :] for i, j in (
            (0, jnp.clip(local + nblocks, 0, nblocks - 1)),
            (1, inside),
            (2, jnp.clip(local - nblocks, 0, nblocks - 1)),
        ))
        end = jnp.where(local < 0, before, jnp.where(local < nblocks, here, after))
        both = block[half:].astype(F32)
        first = jnp.where(below, 0.0, both).astype(BF16)
        second = jnp.where(below, both, 0.0).astype(BF16)
        matrix = jnp.concatenate(
            [
                jnp.concatenate([first, block[:half]], axis=1),
                jnp.concatenate([jnp.zeros_like(first), second], axis=1),
            ],
            axis=0,
        )
        value = values[s]
        inner = jnp.dot(value, matrix, preferred_element_type=F32)
        wide = value.astype(F32)
        left, right = wide[:, :half], wide[:, half:]
        each = left * inner[:, :half] + right * (inner[:, half:] + right * end)
        return jnp.where(s < count_ref[0], each, 0.0)

    total = jnp.zeros((values.shape[1], half), F32)
    forward(0)
    for s in range(slots):
        if s + 1 < slots:
            forward(s + 1)
        total = total + contribution(s)
    out_ref[...] = jnp.sum(total.T, axis=0, keepdims=True)

    for level in range(LEVELS):
        for copy in upper_copies(level):
            copy.wait_send()
    for k in peers:
        for chunk in range(CHUNKS):
            part_copy(chunk, k).wait_send()
        pdiag_copy(k).wait_send()
        own_copy(k, pole).wait_send()
    for d, there, neighbour in sides:

        @pl.when(there)
        def _():
            list_copy(d, neighbour, 1 - d).wait_send()
            hdiag_copy(d, neighbour, 1 - d).wait_send()
            for s in range(slots):
                halo_copy(d, neighbour, 1 - d, s).wait_send()
                for k in peers:
                    fwd_copy(d, s, k, pole).wait_send()


def shards(
    n_pole,
    n_sep,
    diag_inverse,
    coupling,
    ancestor_inverse,
    pole_weight,
    ancestor_bit,
    tile_blocks,
    tile_count,
    orbital_values,
):
    nblocks, _, width, _ = diag_inverse.shape[1:]
    slots, points = orbital_values.shape[1:3]
    half = width // 2
    rows = width // n_pole
    dma = pltpu.SemaphoreType.DMA
    scratch = [
        pltpu.VMEM(diag_inverse.shape[1:], BF16),
        pltpu.VMEM(coupling.shape[1:], BF16),
        pltpu.VMEM(ancestor_inverse.shape[2:], BF16),
        pltpu.VMEM(orbital_values.shape[1:], BF16),
        pltpu.VMEM((5, half, half), BF16),
        pltpu.VMEM((LEVELS, 5, half, half), BF16),
        pltpu.VMEM((LEVELS, 2 * width, 2 * width), BF16),
        pltpu.VMEM((nblocks, width, half), F32),
        pltpu.VMEM((nblocks, half), F32),
        pltpu.VMEM((n_pole, nblocks, rows, half), F32),
        pltpu.VMEM((n_pole, nblocks, rows, half), F32),
        pltpu.VMEM((n_pole, nblocks, half), F32),
        pltpu.VMEM((nblocks, rows, half), BF16),
        pltpu.VMEM((nblocks, width, half), BF16),
        pltpu.VMEM((2, slots, width, half), BF16),
        pltpu.VMEM((3, nblocks, half), F32),
        pltpu.VMEM((2, slots, rows, half), BF16),
        pltpu.VMEM((8, 128), jnp.int32),
        pltpu.VMEM((2, 8, 128), jnp.int32),
        pltpu.SMEM((2, 8, 128), jnp.int32),
        dma((4,)),
        dma((2,)),
        dma((LEVELS, 2)),
        dma((LEVELS, 2)),
        dma((CHUNKS, n_pole)),
        dma((CHUNKS, n_pole)),
        dma((n_pole,)),
        dma((n_pole,)),
        dma((n_pole,)),
        dma((n_pole,)),
        dma((2, slots)),
        dma((2, slots)),
        dma((2,)),
        dma((2,)),
        dma((2, slots, n_pole)),
        dma((2, slots, n_pole)),
        dma((2,)),
        dma((2,)),
    ]
    smem = pl.BlockSpec(memory_space=pltpu.SMEM)
    anywhere = pl.BlockSpec(memory_space=pl.ANY)
    return pl.pallas_call(
        functools.partial(kernel, n_pole, n_sep),
        out_shape=jax.ShapeDtypeStruct((1, points), F32),
        in_specs=[smem] * 4 + [anywhere] * 4,
        out_specs=pl.BlockSpec(memory_space=pltpu.VMEM),
        scratch_shapes=scratch,
        compiler_params=pltpu.CompilerParams(
            collective_id=0, has_side_effects=True, vmem_limit_bytes=60 * 1024 * 1024
        ),
    )(
        pole_weight,
        ancestor_bit,
        tile_blocks,
        tile_count,
        diag_inverse,
        coupling,
        ancestor_inverse,
        orbital_values,
    )


def solution(mesh):
    placed = (
        P("pole", "sep", None, None, None),
        P("pole", "sep", None, None, None),
        P("pole", "sep", None, None, None),
        P("pole", None),
        P("sep"),
        P("sep", None),
        P("sep"),
        P("sep", None, "pole", None),
    )
    return jax.shard_map(
        functools.partial(shards, mesh.shape["pole"], mesh.shape["sep"]),
        mesh=mesh,
        in_specs=placed,
        out_specs=P("sep", "pole"),
        check_vma=False,
    )
```

time: 92.9 us -> 35.7 us (0.38)
  the two profiles are of different devices: /device:TPU:0 before, /device:TPU:11 now
where the time goes in v1:
time: 35.7 us; the launch traced here: 35.6 us
  Pallas kernels  33.7 us (94%)
  local copies, waits for them, and re-layouts  1.24 us (3%)
  between operations  0.66 us (2%)
    pallas_call x1, Pallas kernels, shards(): pl.pallas_call(functools.partial(kernel, n_pole, n_sep), out_shape=jax.Sh...  33.7 us
    unnamed x1, local copies, waits for them, and re-layouts  1.24 us

profile of v1, /device:TPU:11, one launch (start us, length us, event | category | flops | bytes accessed | tf_op | source)
XLA Modules:
  0.0 35.6 jit_solution(15723587143275228803)
XLA Ops:
  0.7 33.7 %shard_map.82 = f32[1,256]{1,0:T(1,128)} custom-call(f32[1,2]{1,0:T(1,128)} %weight_ref.1, s32[8]{0:T(128)} %bit_ref.1, s32[1,6]{1,0:T(1,128)} %blocks_ref.1, s32[1]{0:T(128)S(6)} %copy.10.count_ref, bf16[1,8,2,256,256]{4,3,2,1,0:T(8,128)(2,1)} %diag_hbm.1, bf16[1,8,2,256,256]{4,3,2,1,0:T(8,128)(2,1)} %link_hbm.1, bf16[1,1,2,256,256]{4,3,2,1,0:T(8,128)(2,1)} %upper_hbm.1, ...), custom_call_target="tpu_custom_call" | custom-call | tf_op jit(solution)/shard_map/pallas_call | solution.py:487
  34.3 1.2 %copy.11 = f32[1,256]{1,0:T(1,128)} copy(f32[1,256]{1,0:T(1,128)} %shard_map.82) | data formatting | bytes 2048

commit v2 on v1

--- a/solution.py
+++ b/solution.py
@@ -8,7 +8,8 @@
 from jax.sharding import PartitionSpec as P
 
 LEVELS = 4
-CHUNKS = 2
+CHUNKS = 4
+EARLY = 3
 MESH = pl.DeviceIdType.MESH
 F32 = jnp.float32
 BF16 = jnp.bfloat16
@@ -39,7 +40,8 @@
     full,
     body,
     body_diag,
-    part_send,
+    early,
+    early_recv,
     part_recv,
     part_diag,
     mine,
@@ -54,6 +56,8 @@
     list_sem,
     upper_send_sem,
     upper_recv_sem,
+    early_send_sem,
+    early_recv_sem,
     part_send_sem,
     part_recv_sem,
     pdiag_send_sem,
@@ -208,7 +212,7 @@
         body_diag[pl.ds(b, 1), :] = diagonal(t11)
         return carry
 
-    lax.fori_loop(0, nblocks, fold, 0)
+    lax.fori_loop(0, nblocks, fold, 0, unroll=2)
     loads[2].wait()
 
     for d, there, neighbour in sides:
@@ -217,6 +221,12 @@
         def _():
             list_copy(d, neighbour, d).wait_recv()
             fetch = pltpu.make_async_copy(list_recv.at[d], list_smem.at[d], list_sem.at[d])
+            fetch.start()
+            fetch.wait()
+
+        @pl.when(jnp.logical_not(there))
+        def _():
+            fetch = pltpu.make_async_copy(list_send, list_smem.at[d], list_sem.at[d])
             fetch.start()
             fetch.wait()
 
@@ -242,7 +252,7 @@
                 full[level, 2 * half + r : 3 * half + r, c : c + half] = -imag
                 full[level, 2 * half + r : 3 * half + r, 2 * half + c : 3 * half + c] = real
 
-    def density(b, carry):
+    def density(b):
         real, imag = link[b, 0], link[b, 1]
         middle = jnp.dot(
             jnp.concatenate([real, imag], axis=1), full[bit_ref[b]], preferred_element_type=F32
@@ -251,15 +261,26 @@
         top = nt_dot(middle[:half], crossed)
         low = nt_dot(middle[half:], crossed[half:])
         corner = top[:, :half]
-        body[b, :half, :] += top[:, half:]
-        body[b, half:, :] += jnp.where(above, corner, jnp.where(below, low, 0.5 * corner))
-        body_diag[pl.ds(b, 1), :] += 0.5 * diagonal(low)
-        return carry
+        upper_right = body[b, :half, :] + top[:, half:]
+        corners = body[b, half:, :] + jnp.where(above, corner, jnp.where(below, low, 0.5 * corner))
+        return upper_right, corners, low
+
+    def local_of(d, s):
+        return jnp.clip(list_smem[d, 0, s] - me * nblocks, 0, nblocks - 1)
+
+    def early_copy(s, k):
+        return remote(
+            early.at[s, :, piece(peer(k))],
+            early_recv.at[k, s],
+            early_send_sem.at[s, k],
+            early_recv_sem.at[s, k],
+            {"pole": peer(k)},
+        )
 
     def part_copy(chunk, k):
         at = pl.ds(chunk * per_chunk, per_chunk)
         return remote(
-            part_send.at[k, at],
+            body.at[at, piece(peer(k))],
             part_recv.at[k, at],
             part_send_sem.at[chunk, k],
             part_recv_sem.at[chunk, k],
@@ -271,16 +292,32 @@
             body_diag, part_diag.at[k], pdiag_send_sem.at[k], pdiag_recv_sem.at[k], {"pole": peer(k)}
         )
 
-    for chunk in range(CHUNKS):
-        lax.fori_loop(chunk * per_chunk, (chunk + 1) * per_chunk, density, 0)
+    def halo_copy(d, neighbour, slot, s):
+        return remote(
+            chosen.at[d, s],
+            near.at[slot, s, piece(pole)],
+            halo_send_sem.at[d, s],
+            halo_recv_sem.at[slot, s],
+            {"sep": neighbour},
+        )
+
+    def send_halo(s):
+        for d, there, neighbour in sides:
+
+            @pl.when(there)
+            def _():
+                halo_copy(d, neighbour, 1 - d, s).start()
+
+    def finish_early(s):
+        total = early[s, :, piece(pole), :]
         for k in peers:
-            at = pl.ds(chunk * per_chunk, per_chunk)
-            part_send[k, at] = body[at, piece(peer(k)), :]
-            part_copy(chunk, k).start()
-    for k in peers:
-        pdiag_copy(k).start()
-
-    for chunk in range(CHUNKS):
+            early_copy(s, k).wait_recv()
+            total = total + early_recv[k, s]
+        for d in range(2):
+            chosen[d, s] = total[d].astype(BF16)
+        send_halo(s)
+
+    def finish_part(chunk):
         at = pl.ds(chunk * per_chunk, per_chunk)
         total = body[at, piece(pole), :]
         for k in peers:
@@ -288,23 +325,36 @@
             total = total + part_recv[k, at]
         mine[at] = total.astype(BF16)
 
-    def halo_copy(d, neighbour, slot, s):
-        return remote(
-            chosen.at[d, s],
-            near.at[slot, s, piece(pole)],
-            halo_send_sem.at[d, s],
-            halo_recv_sem.at[slot, s],
-            {"sep": neighbour},
-        )
-
-    for s in range(slots):
-        for d, there, neighbour in sides:
-
-            @pl.when(there)
-            def _():
-                local = jnp.clip(list_smem[d, 0, s] - me * nblocks, 0, nblocks - 1)
-                chosen[d, s] = mine[local]
-                halo_copy(d, neighbour, 1 - d, s).start()
+    for s in range(EARLY):
+        for d in range(2):
+            upper_right, corners, _ = density(local_of(d, s))
+            early[s, d, :half, :] = upper_right
+            early[s, d, half:, :] = corners
+        for k in peers:
+            early_copy(s, k).start()
+        if s > 0:
+            finish_early(s - 1)
+
+    for chunk in range(CHUNKS):
+        for b in range(chunk * per_chunk, (chunk + 1) * per_chunk):
+            upper_right, corners, low = density(b)
+            body[b, :half, :] = upper_right
+            body[b, half:, :] = corners
+            body_diag[b : b + 1, :] += 0.5 * diagonal(low)
+        for k in peers:
+            part_copy(chunk, k).start()
+        if chunk == 0:
+            finish_early(EARLY - 1)
+        else:
+            finish_part(chunk - 1)
+    for k in peers:
+        pdiag_copy(k).start()
+    finish_part(CHUNKS - 1)
+
+    for s in range(EARLY, slots):
+        for d in range(2):
+            chosen[d, s] = mine[local_of(d, s)]
+        send_halo(s)
 
     def own_copy(k, q):
         return remote(
@@ -339,11 +389,6 @@
     loads[3].wait()
     for k in peers:
         own_copy(k, peer(n_pole - k)).wait_recv()
-    for d, there, neighbour in sides:
-
-        @pl.when(there)
-        def _():
-            hdiag_copy(d, neighbour, d).wait_recv()
 
     def fwd_copy(d, s, k, q):
         return remote(
@@ -374,12 +419,6 @@
         local = blocks_ref[0, s] - me * nblocks
         inside = jnp.clip(local, 0, nblocks - 1)
         block = jnp.where(local < 0, near[0, s], jnp.where(local < nblocks, own[inside], near[1, s]))
-        before, here, after = (near_diag[i, pl.ds(j, 1), :] for i, j in (
-            (0, jnp.clip(local + nblocks, 0, nblocks - 1)),
-            (1, inside),
-            (2, jnp.clip(local - nblocks, 0, nblocks - 1)),
-        ))
-        end = jnp.where(local < 0, before, jnp.where(local < nblocks, here, after))
         both = block[half:].astype(F32)
         first = jnp.where(below, 0.0, both).astype(BF16)
         second = jnp.where(below, both, 0.0).astype(BF16)
@@ -394,14 +433,32 @@
         inner = jnp.dot(value, matrix, preferred_element_type=F32)
         wide = value.astype(F32)
         left, right = wide[:, :half], wide[:, half:]
-        each = left * inner[:, :half] + right * (inner[:, half:] + right * end)
+        each = left * inner[:, :half] + right * inner[:, half:]
         return jnp.where(s < count_ref[0], each, 0.0)
+
+    def end_contribution(s):
+        local = blocks_ref[0, s] - me * nblocks
+        before, here, after = (
+            near_diag[i, pl.ds(jnp.clip(local + (1 - i) * nblocks, 0, nblocks - 1), 1), :] for i in range(3)
+        )
+        end = jnp.where(local < 0, before, jnp.where(local < nblocks, here, after))
+        right = values[s, :, half:].astype(F32)
+        return jnp.where(s < count_ref[0], right * right * end, 0.0)
 
     total = jnp.zeros((values.shape[1], half), F32)
     forward(0)
     for s in range(slots):
         if s + 1 < slots:
             forward(s + 1)
+        if s + 1 == slots:
+            for d, there, neighbour in sides:
+
+                @pl.when(there)
+                def _():
+                    hdiag_copy(d, neighbour, d).wait_recv()
+
+            for i in range(slots):
+                total = total + end_contribution(i)
         total = total + contribution(s)
     out_ref[...] = jnp.sum(total.T, axis=0, keepdims=True)
 
@@ -409,6 +466,8 @@
         for copy in upper_copies(level):
             copy.wait_send()
     for k in peers:
+        for s in range(EARLY):
+            early_copy(s, k).wait_send()
         for chunk in range(CHUNKS):
             part_copy(chunk, k).wait_send()
         pdiag_copy(k).wait_send()
@@ -452,7 +511,8 @@
         pltpu.VMEM((LEVELS, 2 * width, 2 * width), BF16),
         pltpu.VMEM((nblocks, width, half), F32),
         pltpu.VMEM((nblocks, half), F32),
-        pltpu.VMEM((n_pole, nblocks, rows, half), F32),
+        pltpu.VMEM((EARLY, 2, width, half), F32),
+        pltpu.VMEM((n_pole, EARLY, 2, rows, half), F32),
         pltpu.VMEM((n_pole, nblocks, rows, half), F32),
         pltpu.VMEM((n_pole, nblocks, half), F32),
         pltpu.VMEM((nblocks, rows, half), BF16),
@@ -467,6 +527,8 @@
         dma((2,)),
         dma((LEVELS, 2)),
         dma((LEVELS, 2)),
+        dma((EARLY, n_pole)),
+        dma((EARLY, n_pole)),
         dma((CHUNKS, n_pole)),
         dma((CHUNKS, n_pole)),
         dma((n_pole,)),

time: 35.7 us -> 32.6 us (0.913)
  Pallas kernels: 33.7 us -> 30.5 us
    pallas_call x1, Pallas kernels: 33.7 us -> 30.5 us  [shards(): pl.pallas_call(functools.partial(kernel, n_pole, n_sep), out_shape=jax.Sh...]
where the time goes in v2:
time: 32.6 us; the launch traced here: 32.4 us
  Pallas kernels  30.5 us (94%)
  local copies, waits for them, and re-layouts  1.24 us (4%)
  between operations  0.66 us (2%)
    pallas_call x1, Pallas kernels, shards(): pl.pallas_call(functools.partial(kernel, n_pole, n_sep), out_shape=jax.Sh...  30.5 us
    unnamed x1, local copies, waits for them, and re-layouts  1.24 us

profile of v2, /device:TPU:11, one launch (start us, length us, event | category | flops | bytes accessed | tf_op | source)
XLA Modules:
  0.0 32.4 jit_solution(14901673442492973624)
XLA Ops:
  0.7 30.5 %shard_map.82 = f32[1,256]{1,0:T(1,128)} custom-call(f32[1,2]{1,0:T(1,128)} %weight_ref.1, s32[8]{0:T(128)} %bit_ref.1, s32[1,6]{1,0:T(1,128)} %blocks_ref.1, s32[1]{0:T(128)S(6)} %copy.10.count_ref, bf16[1,8,2,256,256]{4,3,2,1,0:T(8,128)(2,1)} %diag_hbm.1, bf16[1,8,2,256,256]{4,3,2,1,0:T(8,128)(2,1)} %link_hbm.1, bf16[1,1,2,256,256]{4,3,2,1,0:T(8,128)(2,1)} %upper_hbm.1, ...), custom_call_target="tpu_custom_call" | custom-call | tf_op jit(solution)/shard_map/pallas_call | solution.py:549
  31.2 1.2 %copy.11 = f32[1,256]{1,0:T(1,128)} copy(f32[1,256]{1,0:T(1,128)} %shard_map.82) | data formatting | bytes 2048

commit v3 on v2

--- a/solution.py
+++ b/solution.py
@@ -9,7 +9,7 @@
 
 LEVELS = 4
 CHUNKS = 4
-EARLY = 3
+EARLY = 4
 MESH = pl.DeviceIdType.MESH
 F32 = jnp.float32
 BF16 = jnp.bfloat16
@@ -22,15 +22,18 @@
 def kernel(
     n_pole,
     n_sep,
-    weight_ref,
-    bit_ref,
-    blocks_ref,
+    weight_hbm,
+    bit_hbm,
+    blocks_hbm,
     count_ref,
     diag_hbm,
     link_hbm,
     upper_hbm,
     values_hbm,
     out_ref,
+    weight_ref,
+    bit_ref,
+    blocks_ref,
     diag,
     link,
     upper,
@@ -53,6 +56,7 @@
     list_recv,
     list_smem,
     local_sem,
+    small_sem,
     list_sem,
     upper_send_sem,
     upper_recv_sem,
@@ -110,8 +114,15 @@
             )
         )
     ]
-    for load in loads:
-        load.start()
+    small = [
+        pltpu.make_async_copy(src, dst, small_sem.at[i])
+        for i, (src, dst) in enumerate(
+            ((weight_hbm, weight_ref), (blocks_hbm, blocks_ref), (bit_hbm, bit_ref))
+        )
+    ]
+    loads[0].start()
+    for copy in small:
+        copy.start()
 
     barrier = pltpu.get_barrier_semaphore()
     for k in peers:
@@ -131,6 +142,8 @@
     def diagonal(x):
         return jnp.sum(jnp.where(on, x, 0.0), axis=0, keepdims=True)
 
+    for copy in small:
+        copy.wait()
     wr, wi = weight_ref[0, 0], weight_ref[0, 1]
 
     lane = lax.broadcasted_iota(jnp.int32, list_send.shape, 1)
@@ -140,6 +153,8 @@
     list_send[...] = listed
 
     loads[0].wait()
+    for load in loads[1:]:
+        load.start()
     doubled = []
     for part in range(2):
         g00 = upper[part, :half, :half].astype(F32)
@@ -258,10 +273,9 @@
             jnp.concatenate([real, imag], axis=1), full[bit_ref[b]], preferred_element_type=F32
         ).astype(BF16)
         crossed = jnp.concatenate([imag, real], axis=1)
-        top = nt_dot(middle[:half], crossed)
-        low = nt_dot(middle[half:], crossed[half:])
-        corner = top[:, :half]
-        upper_right = body[b, :half, :] + top[:, half:]
+        product = nt_dot(middle, crossed)
+        corner, low = product[:half, :half], product[half:, half:]
+        upper_right = body[b, :half, :] + product[:half, half:]
         corners = body[b, half:, :] + jnp.where(above, corner, jnp.where(below, low, 0.5 * corner))
         return upper_right, corners, low
 
@@ -502,6 +516,9 @@
     rows = width // n_pole
     dma = pltpu.SemaphoreType.DMA
     scratch = [
+        pltpu.SMEM(pole_weight.shape, F32),
+        pltpu.SMEM(ancestor_bit.shape, jnp.int32),
+        pltpu.SMEM(tile_blocks.shape, jnp.int32),
         pltpu.VMEM(diag_inverse.shape[1:], BF16),
         pltpu.VMEM(coupling.shape[1:], BF16),
         pltpu.VMEM(ancestor_inverse.shape[2:], BF16),
@@ -524,6 +541,7 @@
         pltpu.VMEM((2, 8, 128), jnp.int32),
         pltpu.SMEM((2, 8, 128), jnp.int32),
         dma((4,)),
+        dma((3,)),
         dma((2,)),
         dma((LEVELS, 2)),
         dma((LEVELS, 2)),
@@ -544,12 +562,11 @@
         dma((2,)),
         dma((2,)),
     ]
-    smem = pl.BlockSpec(memory_space=pltpu.SMEM)
-    anywhere = pl.BlockSpec(memory_space=pl.ANY)
+    hbm = pl.BlockSpec(memory_space=pl.ANY)
     return pl.pallas_call(
         functools.partial(kernel, n_pole, n_sep),
         out_shape=jax.ShapeDtypeStruct((1, points), F32),
-        in_specs=[smem] * 4 + [anywhere] * 4,
+        in_specs=[hbm] * 3 + [pl.BlockSpec(memory_space=pltpu.SMEM)] + [hbm] * 4,
         out_specs=pl.BlockSpec(memory_space=pltpu.VMEM),
         scratch_shapes=scratch,
         compiler_params=pltpu.CompilerParams(

time: 32.6 us -> 31.4 us (0.963)
  Pallas kernels: 30.5 us -> 29.3 us
    pallas_call x1, Pallas kernels: 30.5 us -> 29.3 us  [shards(): pl.pallas_call(functools.partial(kernel, n_pole, n_sep), out_shape=jax.Sh...]
where the time goes in v3:
time: 31.4 us; the launch traced here: 31.2 us
  Pallas kernels  29.3 us (93%)
  local copies, waits for them, and re-layouts  1.24 us (4%)
  between operations  0.66 us (2%)
    pallas_call x1, Pallas kernels, shards(): pl.pallas_call(functools.partial(kernel, n_pole, n_sep), out_shape=jax.Sh...  29.3 us
    unnamed x1, local copies, waits for them, and re-layouts  1.24 us

profile of v3, /device:TPU:11, one launch (start us, length us, event | category | flops | bytes accessed | tf_op | source)
XLA Modules:
  0.0 31.2 jit_solution(17474320229197246043)
XLA Ops:
  0.7 29.3 %shard_map.82 = f32[1,256]{1,0:T(1,128)} custom-call(f32[1,2]{1,0:T(1,128)} %weight_hbm.1, s32[8]{0:T(128)} %bit_hbm.1, s32[1,6]{1,0:T(1,128)} %blocks_hbm.1, s32[1]{0:T(128)S(6)} %copy.10.count_ref, bf16[1,8,2,256,256]{4,3,2,1,0:T(8,128)(2,1)} %diag_hbm.1, bf16[1,8,2,256,256]{4,3,2,1,0:T(8,128)(2,1)} %link_hbm.1, bf16[1,1,2,256,256]{4,3,2,1,0:T(8,128)(2,1)} %upper_hbm.1, ...), custom_call_target="tpu_custom_call" | custom-call | tf_op jit(solution)/shard_map/pallas_call | solution.py:566
  30.0 1.2 %copy.11 = f32[1,256]{1,0:T(1,128)} copy(f32[1,256]{1,0:T(1,128)} %shard_map.82) | data formatting | bytes 2048

commit v4 on v3

--- a/solution.py
+++ b/solution.py
@@ -214,20 +214,26 @@
 
     loads[1].wait()
 
-    def fold(b, carry):
-        def term(rows_at, cols_at):
-            real = diag[b, 0, rows_at, cols_at].astype(F32)
-            imag = diag[b, 1, rows_at, cols_at].astype(F32)
-            return wr * imag + wi * real
-
-        low, high = pl.ds(0, half), pl.ds(half, half)
-        t00, t01, t10, t11 = term(low, low), term(low, high), term(high, low), term(high, high)
-        body[b, :half, :] = t01 + t10.T
-        body[b, half:, :] = jnp.where(above, t00 + t00.T, jnp.where(below, t11 + t11.T, t00))
-        body_diag[pl.ds(b, 1), :] = diagonal(t11)
+    def fold(pair, carry):
+        def folded(b):
+            def term(rows_at, cols_at):
+                real = diag[b, 0, rows_at, cols_at].astype(F32)
+                imag = diag[b, 1, rows_at, cols_at].astype(F32)
+                return wr * imag + wi * real
+
+            low, high = pl.ds(0, half), pl.ds(half, half)
+            t00, t01, t10, t11 = term(low, low), term(low, high), term(high, low), term(high, high)
+            corners = jnp.where(above, t00 + t00.T, jnp.where(below, t11 + t11.T, t00))
+            return t01 + t10.T, corners, diagonal(t11)
+
+        at = [2 * pair, 2 * pair + 1]
+        for b, (upper_right, corners, end) in zip(at, [folded(b) for b in at]):
+            body[b, :half, :] = upper_right
+            body[b, half:, :] = corners
+            body_diag[pl.ds(b, 1), :] = end
         return carry
 
-    lax.fori_loop(0, nblocks, fold, 0, unroll=2)
+    lax.fori_loop(0, nblocks // 2, fold, 0)
     loads[2].wait()
 
     for d, there, neighbour in sides:
@@ -267,13 +273,12 @@
                 full[level, 2 * half + r : 3 * half + r, c : c + half] = -imag
                 full[level, 2 * half + r : 3 * half + r, 2 * half + c : 3 * half + c] = real
 
-    def density(b):
-        real, imag = link[b, 0], link[b, 1]
-        middle = jnp.dot(
-            jnp.concatenate([real, imag], axis=1), full[bit_ref[b]], preferred_element_type=F32
-        ).astype(BF16)
-        crossed = jnp.concatenate([imag, real], axis=1)
-        product = nt_dot(middle, crossed)
+    def middle_of(b):
+        both = jnp.concatenate([link[b, 0], link[b, 1]], axis=1)
+        return jnp.dot(both, full[bit_ref[b]], preferred_element_type=F32).astype(BF16)
+
+    def density(b, middle):
+        product = nt_dot(middle, jnp.concatenate([link[b, 1], link[b, 0]], axis=1))
         corner, low = product[:half, :half], product[half:, half:]
         upper_right = body[b, :half, :] + product[:half, half:]
         corners = body[b, half:, :] + jnp.where(above, corner, jnp.where(below, low, 0.5 * corner))
@@ -339,28 +344,30 @@
             total = total + part_recv[k, at]
         mine[at] = total.astype(BF16)
 
-    for s in range(EARLY):
-        for d in range(2):
-            upper_right, corners, _ = density(local_of(d, s))
-            early[s, d, :half, :] = upper_right
-            early[s, d, half:, :] = corners
-        for k in peers:
-            early_copy(s, k).start()
-        if s > 0:
-            finish_early(s - 1)
-
-    for chunk in range(CHUNKS):
-        for b in range(chunk * per_chunk, (chunk + 1) * per_chunk):
-            upper_right, corners, low = density(b)
-            body[b, :half, :] = upper_right
-            body[b, half:, :] = corners
-            body_diag[b : b + 1, :] += 0.5 * diagonal(low)
-        for k in peers:
-            part_copy(chunk, k).start()
-        if chunk == 0:
-            finish_early(EARLY - 1)
+    groups = [[local_of(d, s) for d in range(2)] for s in range(EARLY)]
+    groups += [list(range(c * per_chunk, (c + 1) * per_chunk)) for c in range(CHUNKS)]
+    following = [middle_of(b) for b in groups[0]]
+    for g, group in enumerate(groups):
+        middles = following
+        following = [middle_of(b) for b in groups[g + 1]] if g + 1 < len(groups) else []
+        results = [density(b, middle) for b, middle in zip(group, middles)]
+        if g < EARLY:
+            for d, (upper_right, corners, _) in enumerate(results):
+                early[g, d, :half, :] = upper_right
+                early[g, d, half:, :] = corners
+            for k in peers:
+                early_copy(g, k).start()
         else:
-            finish_part(chunk - 1)
+            for b, (upper_right, corners, low) in zip(group, results):
+                body[b, :half, :] = upper_right
+                body[b, half:, :] = corners
+                body_diag[b : b + 1, :] += 0.5 * diagonal(low)
+            for k in peers:
+                part_copy(g - EARLY, k).start()
+        if 1 <= g <= EARLY:
+            finish_early(g - 1)
+        elif g > EARLY:
+            finish_part(g - EARLY - 1)
     for k in peers:
         pdiag_copy(k).start()
     finish_part(CHUNKS - 1)

time: 31.4 us -> 30.9 us (0.984)
  Pallas kernels: 29.3 us -> 28.8 us
    pallas_call x1, Pallas kernels: 29.3 us -> 28.8 us  [shards(): pl.pallas_call(functools.partial(kernel, n_pole, n_sep), out_shape=jax.Sh...]
where the time goes in v4:
time: 30.9 us; the launch traced here: 30.7 us
  Pallas kernels  28.8 us (93%)
  local copies, waits for them, and re-layouts  1.24 us (4%)
  between operations  0.66 us (2%)
    pallas_call x1, Pallas kernels, shards(): pl.pallas_call(functools.partial(kernel, n_pole, n_sep), out_shape=jax.Sh...  28.8 us
    unnamed x1, local copies, waits for them, and re-layouts  1.24 us

profile of v4, /device:TPU:11, one launch (start us, length us, event | category | flops | bytes accessed | tf_op | source)
XLA Modules:
  0.0 30.7 jit_solution(10038610652075602250)
XLA Ops:
  0.7 28.8 %shard_map.82 = f32[1,256]{1,0:T(1,128)} custom-call(f32[1,2]{1,0:T(1,128)} %weight_hbm.1, s32[8]{0:T(128)} %bit_hbm.1, s32[1,6]{1,0:T(1,128)} %blocks_hbm.1, s32[1]{0:T(128)S(6)} %copy.10.count_ref, bf16[1,8,2,256,256]{4,3,2,1,0:T(8,128)(2,1)} %diag_hbm.1, bf16[1,8,2,256,256]{4,3,2,1,0:T(8,128)(2,1)} %link_hbm.1, bf16[1,1,2,256,256]{4,3,2,1,0:T(8,128)(2,1)} %upper_hbm.1, ...), custom_call_target="tpu_custom_call" | custom-call | tf_op jit(solution)/shard_map/pallas_call | solution.py:573
  29.5 1.2 %copy.11 = f32[1,256]{1,0:T(1,128)} copy(f32[1,256]{1,0:T(1,128)} %shard_map.82) | data formatting | bytes 2048
